TPU v7x, 256 devices: a whole 4x4x8 slice. The times are simulated.
256 devices in a mesh: leaf: 64 (over z, y, core), sub: 4 (over x).
Axes of the slice: x: 4, y: 4, z: 8, core: 2. Of those that a mesh axis runs over, the one named last changes fastest.
Arguments:
- coupling: float32 [524288, 4, 128], P(('leaf', 'sub')), may hold values from -40 to 40, as said below
- weights: float32 [524288], P(('leaf', 'sub')), may hold values from 0.3 to 3, as said below
- rhs: float32 [524288, 128], P(('leaf', 'sub')), may hold values from -6 to 6
- order: int32 [256, 2048], P(('leaf', 'sub')), may hold values from 0 to 2047, each once within a row
Outputs:
- applied: float32 [524288, 4, 128], P(('leaf', 'sub'))
- answer: float32 [524288, 128], P(('leaf', 'sub'))
Inputs may be any that keep to these rules, and one draw needn't show every extreme that they name: coupling and weights are finite and bounded as stated. weights are positive. `order`: each row is a permutation of 0 to 2047.
All inputs are finite; a program needn't handle non-finite values.
Results may differ from a plain program's by a relative error of at most 0.00024.
Values sent between devices are 32-bit elements; how exact they have to be, the bound alone decides.
A program may use at most 128 MiB of HBM per device.

v0:
```python
import jax
import jax.numpy as jnp
from jax import lax
from jax.experimental import pallas as pl
from jax.experimental.pallas import tpu as pltpu
from jax.sharding import PartitionSpec as P

MESH = pl.DeviceIdType.MESH
F32 = jnp.float32
BF = jnp.bfloat16
ROWS = 2048
CAP = 128
AGENTS = 524288
CHUNK = 256
EARLY = 1024


def split(x):
    head = x.astype(BF)
    return head, (x - head.astype(F32)).astype(BF)


def dot3(a, b, contract=((1,), (0,))):
    def one(p, q):
        return lax.dot_general(p, q, (contract, ((), ())), preferred_element_type=F32)

    return one(a[0], b[0]) + (one(a[0], b[1]) + one(a[1], b[0]))


def dot_full(a, b):
    return jnp.dot(a, b, precision=lax.Precision.HIGHEST, preferred_element_type=F32)


def sub_bcast(v, i):
    return jnp.broadcast_to(v[i : i + 1, :], (8, 128))


def lane_bcast(v, j):
    return jnp.broadcast_to(v[:, j : j + 1], (8, 128))


def lane_full(v, j):
    return jnp.maximum(lane_bcast(v, j), -3e38)


def recip(x):
    r = pltpu.reciprocal(x, approx=True)
    return r * (2.0 - x * r)


def eliminate_panel(cols, rows, ahead, off, lane, sub):
    cols, ahead = list(cols), list(ahead)
    out = jnp.where(
        (lane >= off) & (lane < off + 8), jnp.where(lane - off == sub, 1.0, 0.0), rows
    )
    for i in range(0, 8, 2):
        ci, cj = cols[i], cols[i + 1]
        a, b = sub_bcast(ci, i), sub_bcast(cj, i)
        b2, c = sub_bcast(ci, i + 1), sub_bcast(cj, i + 1)
        inv_det = recip(a * c - b * b2)
        n0 = jnp.where(sub == i, -c, jnp.where(sub == i + 1, b2, ci * c - cj * b2))
        n1 = jnp.where(sub == i, b, jnp.where(sub == i + 1, -a, cj * a - ci * b))
        f0, f1 = n0 * inv_det, n1 * inv_det
        keep = (sub != i) & (sub != i + 1)

        def update(v):
            return jnp.where(keep, v, 0.0) - (f0 * sub_bcast(v, i) + f1 * sub_bcast(v, i + 1))

        for j in range(i + 2, 8):
            cols[j] = update(cols[j])
        out = update(out)
        ahead = [update(v) for v in ahead]
    return out, ahead


def rank8(v, cols, rows):
    t = [cols[j] * rows[j] for j in range(8)]
    return v - (((t[0] + t[1]) + (t[2] + t[3])) + ((t[4] + t[5]) + (t[6] + t[7])))


def invert(matrix, block=8):
    s = [matrix[8 * q : 8 * q + 8, :] for q in range(16)]
    lane = lax.broadcasted_iota(jnp.int32, (8, 128), 1)
    sub = lax.broadcasted_iota(jnp.int32, (8, 128), 0)
    for first in range(0, 16, block):
        cols = [lane_full(s[first], 8 * first + j) for j in range(8)]
        for k in range(block):
            off = 8 * (first + k)
            inside = (lane >= off) & (lane < off + 8)
            last = k == block - 1
            rows = s[first + k]
            ahead = [] if last else [lane_full(rows, off + 8 + j) for j in range(8)]
            u, ahead = eliminate_panel(cols, rows, ahead, off, lane, sub)
            us = [sub_bcast(u, j) for j in range(8)]
            if not last:
                v = s[first + k + 1]
                lead = [lane_bcast(v, off + j) for j in range(8)]
                cols = [
                    rank8(lane_bcast(v, off + 8 + j), lead, [sub_bcast(ahead[j], i) for i in range(8)])
                    for j in range(8)
                ]
                s[first + k + 1] = rank8(jnp.where(inside, 0.0, v), lead, us)
            far = range(block - 1) if last else [(k + 2 + m) % block for m in range(block - 2)]
            for t in far:
                v = s[first + t]
                lead = [lane_bcast(v, off + j) for j in range(8)]
                s[first + t] = rank8(jnp.where(inside, 0.0, v), lead, us)
            s[first + k] = u
        rest = [(first + block + m) % 16 for m in range(16 - block)]
        left = jnp.concatenate([s[q] for q in rest], axis=0)
        left_lane = lax.broadcasted_iota(jnp.int32, left.shape, 1)
        inside = (left_lane >= 8 * first) & (left_lane < 8 * (first + block))
        parts = [jnp.zeros((8, 128), F32)] * 16
        parts[first : first + block] = s[first : first + block]
        wide = jnp.concatenate(parts, axis=0)
        new = jnp.where(inside, 0.0, left) - dot_full(jnp.where(inside, left, 0.0), wide)
        for m, q in enumerate(rest):
            s[q] = new[8 * m : 8 * m + 8]
    return jnp.concatenate(s, axis=0)


def kernel(
    order, w_s, w_v, coup_hbm, coup_rows_hbm, rhs_hbm, rhs_rows_hbm,
    applied_out, answer_out, a0h_out, a0l_out, p0h, p0l,
    coup, coup_rows, rhs, rhs_rows, in_sem, applied, answer, a0h, a0l, out_sem,
    xh, xl, wh, wl,
    ga, ra, rsa, pa, fa,
    gb, rb, rsb, pb, fb,
    gc, rc, rsc, pc, fc, fd,
    z1s, z1r, z1ps, z1pr, p2,
    z2s, z2r, z2ps, z2pr, p1,
    z4s, z4r, z4bs, z4br,
    ph, plo, mt,
    core_sem, rsa_sem, aga_sem, rsb_sem, agb_sem, rsc_sem, agc_sem, agd_sem, z_sem,
):
    leaf = lax.axis_index("leaf")
    x = lax.axis_index("sub")
    z, y, c = leaf // 8, (leaf // 2) % 4, leaf % 2
    me = x * 4 + y

    def device(px, py, pz, pc):
        return (pz * 8 + py * 2 + pc, px)

    plane = []
    for dx in range(4):
        for dy in range(4):
            if (dx, dy) != (0, 0):
                plane.append((abs(2 - dx) + abs(2 - dy), dx, dy))
    plane = [((x + dx) % 4, (y + dy) % 4) for _, dx, dy in sorted(plane)]
    core_id = device(x, y, z, 1 - c)
    plane_ids = [device(px, py, z, c) for px, py in plane]
    plane_q = [px * 4 + py for px, py in plane]

    def z_flip(bit):
        return device(x, y, z + bit - 2 * bit * ((z // bit) % 2), c)

    z_ids = [z_flip(1), z_flip(2), z_flip(4)]

    quarter = ROWS // 4
    loads = []
    for i in range(4):
        at, at4 = pl.ds(quarter * i, quarter), pl.ds(4 * quarter * i, 4 * quarter)
        loads.append(pltpu.make_async_copy(coup_hbm.at[at4], coup.at[at4], in_sem.at[i]))
        loads.append(pltpu.make_async_copy(rhs_hbm.at[at], rhs.at[at], in_sem.at[4 + i]))
    loads.append(pltpu.make_async_copy(coup_rows_hbm, coup_rows, in_sem.at[8]))
    loads.append(pltpu.make_async_copy(rhs_rows_hbm, rhs_rows, in_sem.at[9]))
    for copy in loads[:8]:
        copy.start()

    barrier = pltpu.get_barrier_semaphore()
    everyone = plane_ids + [core_id] + z_ids
    for d in everyone:
        pl.semaphore_signal(barrier, inc=1, device_id=d, device_id_type=MESH)

    def send(src, dst, sems, i, d):
        copy = pltpu.make_async_remote_copy(
            src_ref=src, dst_ref=dst, send_sem=sems.at[0, i], recv_sem=sems.at[1, i],
            device_id=d, device_id_type=MESH,
        )
        copy.start()
        return copy

    def wait(copies):
        for copy in copies:
            copy.wait()

    def scatter(src, dst, sems):
        return [send(src.at[q], dst.at[i], sems, i, d) for i, (q, d) in enumerate(zip(plane_q, plane_ids))]

    def gather(src, dst, sems):
        return [send(src, dst.at[me], sems, i, d) for i, d in enumerate(plane_ids)]

    weight_cols = jnp.concatenate([w_v[...], jnp.zeros((112, 128), F32)], axis=0).T
    for g in range(16):
        if g % 4 == 0:
            wait(loads[g // 2 : g // 2 + 2])
        r0 = 128 * g
        col = jnp.broadcast_to(weight_cols[:, g : g + 1], (128, 128))
        for k in range(4):
            j = 3 - k
            basis = coup[pl.ds(4 * r0 + k, 128, stride=4), :]
            h, l = split(basis)
            xh[r0 : r0 + 128, 128 * j : 128 * j + 128] = h
            xl[r0 : r0 + 128, 128 * j : 128 * j + 128] = l
            h, l = split(basis * col)
            wh[r0 : r0 + 128, 128 * j : 128 * j + 128] = h
            wl[r0 : r0 + 128, 128 * j : 128 * j + 128] = l
        h, l = split(rhs[r0 : r0 + 128, :])
        xh[r0 : r0 + 128, 512:640] = h
        xl[r0 : r0 + 128, 512:640] = l

    for copy in loads[8:]:
        copy.start()

    def gram(a0, a1, b0, b1):
        return dot3(
            (wh[:, a0:a1], wl[:, a0:a1]), (xh[:, b0:b1], xl[:, b0:b1]), ((0,), (0,))
        )

    def pieces(value):
        return value.reshape(16, 8, 128)

    def put(ref, first, value):
        for k in range(value.shape[1] // 128):
            ref[:, first + k] = pieces(value[:, 128 * k : 128 * k + 128])

    put(ga, 0, gram(0, 128, 0, 256))
    pl.semaphore_wait(barrier, len(everyone))
    core_a = send(ga, ra, core_sem, 0, core_id)
    put(gb, 0, gram(0, 128, 256, 640))
    core_a.wait()
    ga[...] = ga[...] + ra[...]
    rs_a = scatter(ga, rsa, rsa_sem)
    put(gb, 3, gram(128, 256, 128, 256))
    core_b = send(gb, rb, core_sem, 1, core_id)
    m = gram(128, 256, 256, 640)
    for k in range(3):
        gc[0, :, k] = pieces(m[:, 128 * k : 128 * k + 128])
    core_b.wait()
    gb[...] = gb[...] + rb[...]
    rs_b = scatter(gb, rsb, rsb_sem)
    m = gram(256, 512, 256, 640)
    gc[0, :, 3] = pieces(m[:128, :128])
    gc[1, :, 0] = pieces(m[:128, 128:256])
    gc[1, :, 1] = pieces(m[:128, 256:])
    gc[1, :, 2] = pieces(m[128:, 128:256])
    gc[1, :, 3] = pieces(m[128:, 256:])
    core_c = send(gc.at[1 - c], rc, core_sem, 2, core_id)
    wait(rs_a)
    pa[...] = ga[me] + jnp.sum(rsa[...], axis=0)
    fa[me] = pa[...]
    ag_a = gather(pa, fa, aga_sem)
    core_c.wait()
    rc[...] = rc[...] + gc[c]
    rs_c = scatter(rc, rsc, rsc_sem)
    wait(rs_b)
    pb[...] = gb[me] + jnp.sum(rsb[...], axis=0)
    fb[me] = pb[...]
    ag_b = gather(pb, fb, agb_sem)

    wait(loads[8:])

    def permute(t, carry):
        for u in range(8):
            i = t * 8 + u
            r = order[i]
            s = w_s[r]
            applied[pl.ds(pl.multiple_of(4 * i, 4), 4), :] = coup_rows[r] * s
            answer[pl.ds(i, 1), :] = rhs_rows[r] * s
        return carry

    lax.fori_loop(0, EARLY // 8, permute, 0)

    eye = jnp.where(
        lax.broadcasted_iota(jnp.int32, (128, 128), 0)
        == lax.broadcasted_iota(jnp.int32, (128, 128), 1),
        1.0,
        0.0,
    )

    def block(ref, k):
        return ref[:, k].reshape(128, 128)

    def blocks(ref, first, count):
        return jnp.concatenate([block(ref, first + k) for k in range(count)], axis=1)

    def inverse_of(lead, nodes):
        scale = nodes / AGENTS
        return invert(eye + lead * scale) * scale

    def offset(level):
        return sum(128 * (k + 1) for k in range(3, level, -1))

    def keep(level, p):
        h, l = split(p)
        ph[:, offset(level) : offset(level) + p.shape[1]] = h
        plo[:, offset(level) : offset(level) + p.shape[1]] = l

    def subtract(level):
        cut = slice(offset(level), offset(level) + 128 * (level + 1))

        def body(t, carry):
            r0 = pl.multiple_of(t * CHUNK, CHUNK)
            lead = split(applied[pl.ds(4 * r0 + level, CHUNK, stride=4), :])
            change = dot3(lead, (ph[:, cut], plo[:, cut]))
            for k in range(level):
                at = pl.ds(4 * r0 + level - 1 - k, CHUNK, stride=4)
                applied[at, :] = applied[at, :] - change[:, 128 * k : 128 * k + 128]
            at = pl.ds(r0, CHUNK)
            answer[at, :] = answer[at, :] - change[:, 128 * level :]
            return carry

        lax.fori_loop(0, ROWS // CHUNK, body, 0)

    def turn(ref, first, count):
        for k in range(count):
            mt[128 * k : 128 * k + 128, :] = block(ref, first + k).T

    def reduced(inverse, count, lead, rest):
        own = [mt[pl.ds(pl.multiple_of(128 * k + 8 * me, 8), 8), :] for k in range(count)]
        left = dot_full(jnp.concatenate([mt[0:128, :]] + own, axis=0), inverse)
        return dot_full(left[:128], lead), dot_full(left[128:], rest)

    wait(ag_a)
    turn(fa, 1, 1)
    inverse = inverse_of(block(fa, 0), 8.0)
    wait(rs_c)
    pc[c] = rc[me] + jnp.sum(rsc[...], axis=0)
    core_p = send(pc.at[c], pc.at[c], core_sem, 3, core_id)
    wait(ag_b)
    for k in range(2):
        mt[128 * k + 128 : 128 * k + 256, :] = block(fb, k).T
    m32 = block(fa, 1)
    rest = blocks(fb, 0, 3)
    full, part = reduced(inverse, 3, m32, rest)
    core_p.wait()
    where = [(0, 0), (0, 1), (0, 2), (1, 0), (1, 1), (1, 2), (2, 1), (2, 2)]
    for k, (i, j) in enumerate(where):
        z1ps[k] = pc[k // 4, k % 4] - part[8 * i : 8 * i + 8, 128 * j : 128 * j + 128]
    z1p = send(z1ps, z1pr, z_sem, 1, z_ids[0])
    z1s[...] = block(fb, 3) - full
    z1 = send(z1s, z1r, z_sem, 0, z_ids[0])
    keep(3, dot_full(inverse, jnp.concatenate([m32, rest], axis=1)))
    lax.fori_loop(EARLY // 8, ROWS // 8, permute, 0)
    z1p.wait()
    p2[...] = z1ps[...] + z1pr[...]
    fc[me] = p2[0:4]
    ag_c = gather(p2.at[0:4], fc, agc_sem)

    z1.wait()
    inverse = inverse_of(z1s[...] + z1r[...], 4.0)
    subtract(3)
    wait(ag_c)
    turn(fc, 0, 2)
    m21 = block(fc, 0)
    rest = blocks(fc, 1, 2)
    full, part = reduced(inverse, 2, m21, rest)
    for k, (i, j) in enumerate([(0, 0), (0, 1), (1, 0), (1, 1)]):
        z2ps[k] = p2[4 + k] - part[8 * i : 8 * i + 8, 128 * j : 128 * j + 128]
    z2p = send(z2ps, z2pr, z_sem, 3, z_ids[1])
    z2s[...] = block(fc, 3) - full
    z2 = send(z2s, z2r, z_sem, 2, z_ids[1])
    keep(2, dot_full(inverse, jnp.concatenate([m21, rest], axis=1)))
    subtract(2)
    z2p.wait()
    p1[...] = z2ps[...] + z2pr[...]
    fd[me] = p1[...]
    ag_d = gather(p1, fd, agd_sem)

    z2.wait()
    inverse = inverse_of(z2s[...] + z2r[...], 2.0)
    wait(ag_d)
    turn(fd, 0, 1)
    m1 = blocks(fd, 0, 2)
    m0 = blocks(fd, 2, 2) - dot_full(dot_full(mt[0:128, :], inverse), m1)
    z4s[...] = m0[:, :128]
    z4 = send(z4s, z4r, z_sem, 4, z_ids[2])
    z4bs[...] = m0[:, 128:]
    z4b = send(z4bs, z4br, z_sem, 5, z_ids[2])
    keep(1, dot_full(inverse, m1))
    subtract(1)
    h, l = split(applied[pl.ds(0, ROWS, stride=4), :])
    a0h[...] = h
    a0l[...] = l
    outs = [
        pltpu.make_async_copy(a, b, out_sem.at[i])
        for i, (a, b) in enumerate(
            [(applied, applied_out), (answer, answer_out), (a0h, a0h_out), (a0l, a0l_out)]
        )
    ]
    for copy in outs:
        copy.start()

    z4.wait()
    inverse = inverse_of(z4s[...] + z4r[...], 1.0)
    z4b.wait()
    h, l = split(dot_full(inverse, z4bs[...] + z4br[...]))
    p0h[...] = h
    p0l[...] = l
    wait(outs)


PARTS = 8


def finish_kernel(applied_in, answer_in, a0h, a0l, p0h, p0l, applied_out, answer_out, ans, sem):
    rows = ROWS // PARTS
    outs = []
    for i in range(PARTS):
        at4 = pl.ds(4 * rows * i, 4 * rows)
        outs.append(pltpu.make_async_copy(applied_in.at[at4], applied_out.at[at4], sem.at[0, i]))
        outs[-1].start()
    for i in range(PARTS):
        at = pl.ds(rows * i, rows)
        ans[at, :] = answer_in[at, :] - dot3((a0h[at, :], a0l[at, :]), (p0h[...], p0l[...]))
        outs.append(pltpu.make_async_copy(ans.at[at], answer_out.at[at], sem.at[1, i]))
        outs[-1].start()
    for copy in outs:
        copy.wait()


def local(coupling, weights, rhs, order):
    def vmem(*shape, dtype=F32):
        return pltpu.VMEM(shape, dtype)

    def sems(n):
        return pltpu.SemaphoreType.DMA((2, n))

    whole = pl.BlockSpec(memory_space=pltpu.VMEM)
    scalar = pl.BlockSpec(memory_space=pltpu.SMEM)
    anywhere = pl.BlockSpec(memory_space=pl.ANY)
    results = [
        jax.ShapeDtypeStruct((4 * ROWS, CAP), F32),
        jax.ShapeDtypeStruct((ROWS, CAP), F32),
    ]
    last = [jax.ShapeDtypeStruct((ROWS, CAP), BF)] * 2 + [jax.ShapeDtypeStruct((CAP, CAP), BF)] * 2

    def in_hbm(v):
        return pltpu.with_memory_space_constraint(v, pltpu.HBM)

    state = pl.pallas_call(
        kernel,
        in_specs=[scalar, scalar, whole, anywhere, anywhere, anywhere, anywhere],
        out_specs=[anywhere] * 4 + [whole] * 2,
        out_shape=results + last,
        scratch_shapes=[
            vmem(4 * ROWS, CAP), vmem(ROWS, 4, CAP), vmem(ROWS, CAP), vmem(ROWS, 1, CAP),
            pltpu.SemaphoreType.DMA((10,)),
            vmem(4 * ROWS, CAP), vmem(ROWS, CAP), vmem(ROWS, CAP, dtype=BF), vmem(ROWS, CAP, dtype=BF),
            pltpu.SemaphoreType.DMA((4,)),
            vmem(ROWS, 640, dtype=BF), vmem(ROWS, 640, dtype=BF),
            vmem(ROWS, 512, dtype=BF), vmem(ROWS, 512, dtype=BF),
            vmem(16, 2, 8, 128), vmem(16, 2, 8, 128), vmem(15, 2, 8, 128), vmem(2, 8, 128), vmem(16, 2, 8, 128),
            vmem(16, 4, 8, 128), vmem(16, 4, 8, 128), vmem(15, 4, 8, 128), vmem(4, 8, 128), vmem(16, 4, 8, 128),
            vmem(2, 16, 4, 8, 128), vmem(16, 4, 8, 128), vmem(15, 4, 8, 128), vmem(2, 4, 8, 128),
            vmem(16, 4, 8, 128), vmem(16, 4, 8, 128),
            vmem(128, 128), vmem(128, 128), vmem(8, 8, 128), vmem(8, 8, 128), vmem(8, 8, 128),
            vmem(128, 128), vmem(128, 128), vmem(4, 8, 128), vmem(4, 8, 128), vmem(4, 8, 128),
            vmem(128, 128), vmem(128, 128), vmem(128, 128), vmem(128, 128),
            vmem(128, 1280, dtype=BF), vmem(128, 1280, dtype=BF), vmem(384, 128),
            sems(4), sems(15), sems(15), sems(15), sems(15), sems(15), sems(15), sems(15), sems(6),
        ],
        compiler_params=pltpu.CompilerParams(
            collective_id=0, has_side_effects=True, vmem_limit_bytes=44 * 2**20
        ),
        name="hodlr",
    )(
        in_hbm(order.reshape(ROWS)),
        in_hbm(weights),
        in_hbm(weights.reshape(ROWS // 128, 128)),
        in_hbm(coupling.reshape(4 * ROWS, CAP)),
        in_hbm(coupling),
        in_hbm(rhs),
        in_hbm(rhs.reshape(ROWS, 1, CAP)),
    )
    applied, answer = pl.pallas_call(
        finish_kernel,
        in_specs=[anywhere] + [whole] * 5,
        out_specs=[anywhere, anywhere],
        out_shape=results,
        scratch_shapes=[vmem(ROWS, CAP), sems(PARTS)],
        compiler_params=pltpu.CompilerParams(vmem_limit_bytes=16 * 2**20),
        name="finish",
    )(*state)
    return applied.reshape(ROWS, 4, CAP), answer


def solution(mesh):
    rows = ("leaf", "sub")
    return jax.shard_map(
        local,
        mesh=mesh,
        in_specs=(P(rows, None, None), P(rows), P(rows, None), P(rows, None)),
        out_specs=(P(rows, None, None), P(rows, None)),
        check_vma=False,
    )
```

profile of v0, /device:TPU:24, one launch (start us, length us, event | category | flops | bytes accessed | tf_op | source)
XLA Modules:
  0.0 63.2 jit_solution(847600218323712400)
XLA Ops:
  0.6 59.9 %hodlr.1 = (f32[8192,128]{1,0:T(8,128)S(1)}, f32[2048,128]{1,0:T(8,128)S(1)}, bf16[2048,128]{1,0:T(8,128)(2,1)S(1)}, bf16[2048,128]{1,0:T(8,128)(2,1)S(1)}, bf16...) custom-call(s32[2048]{0:T(1024)} %bitcast.8, f32[2048]{0:T(1024)} %w_s.1, f32[16,128]{1,0:T(8,128)} %bitcast.7, ...), custom_call_target="tpu_custom_call" | custom-call | tf_op jit(solution)/shard_map/hodlr/pallas_call | solution.py:441
  60.6 2.5 %finish.1 = (f32[8192,128]{1,0:T(8,128)}, f32[2048,128]{1,0:T(8,128)}) custom-call(f32[8192,128]{1,0:T(8,128)S(1)} %get-tuple-element.10.applied_in, f32[2048,128]{1,0:T(8,128)S(1)} %get-tuple-element.11.answer_in, bf16[2048,128]{1,0:T(8,128)(2,1)S(1)} %get-tuple-element.12.a0h, bf16[2048,128]{1,0:T(8,128)(2,1)S(1)} %get-tuple-element.13.a0l, ...), custom_call_target="tpu_custom_call" | custom-call | tf_op jit(solution)/shard_map/finish/pallas_call | solution.py:476
where the time goes:
time: 63.3 us; the launch traced here: 63.2 us
  Pallas kernels  62.4 us (99%)
  between operations  0.82 us (1%)
    pallas_call x1, Pallas kernels, local(): pl.pallas_call(kernel, in_specs=[scalar, scalar, whole, anywhere, anywher...  59.9 us
    pallas_call x1, Pallas kernels, local(): pl.pallas_call(finish_kernel, in_specs=[anywhere] + [whole] * 5, out_spec...  2.45 us

commit v1 on v0

--- a/solution.py
+++ b/solution.py
@@ -12,7 +12,8 @@
 CAP = 128
 AGENTS = 524288
 CHUNK = 256
-EARLY = 1024
+EARLY = 1280
+LATER = 6
 
 
 def split(x):
@@ -120,9 +121,9 @@
 
 
 def kernel(
-    order, w_s, w_v, coup_hbm, coup_rows_hbm, rhs_hbm, rhs_rows_hbm,
+    order_hbm, w_hbm, wv_hbm, coup_hbm, coup_rows_hbm, rhs_hbm, rhs_rows_hbm,
     applied_out, answer_out, a0h_out, a0l_out, p0h, p0l,
-    coup, coup_rows, rhs, rhs_rows, in_sem, applied, answer, a0h, a0l, out_sem,
+    order, w_s, w_v, coup, coup_rows, rhs, rhs_rows, in_sem, applied, answer, a0h, a0l, out_sem,
     xh, xl, wh, wl,
     ga, ra, rsa, pa, fa,
     gb, rb, rsb, pb, fb,
@@ -164,8 +165,12 @@
         loads.append(pltpu.make_async_copy(rhs_hbm.at[at], rhs.at[at], in_sem.at[4 + i]))
     loads.append(pltpu.make_async_copy(coup_rows_hbm, coup_rows, in_sem.at[8]))
     loads.append(pltpu.make_async_copy(rhs_rows_hbm, rhs_rows, in_sem.at[9]))
+    weight_load = pltpu.make_async_copy(wv_hbm, w_v, in_sem.at[10])
+    weight_load.start()
     for copy in loads[:8]:
         copy.start()
+    loads.append(pltpu.make_async_copy(order_hbm, order, in_sem.at[11]))
+    loads.append(pltpu.make_async_copy(w_hbm, w_s, in_sem.at[12]))
 
     barrier = pltpu.get_barrier_semaphore()
     everyone = plane_ids + [core_id] + z_ids
@@ -190,6 +195,7 @@
     def gather(src, dst, sems):
         return [send(src, dst.at[me], sems, i, d) for i, d in enumerate(plane_ids)]
 
+    weight_load.wait()
     weight_cols = jnp.concatenate([w_v[...], jnp.zeros((112, 128), F32)], axis=0).T
     for g in range(16):
         if g % 4 == 0:
@@ -296,7 +302,7 @@
         ph[:, offset(level) : offset(level) + p.shape[1]] = h
         plo[:, offset(level) : offset(level) + p.shape[1]] = l
 
-    def subtract(level):
+    def subtract(level, start=0, end=ROWS // CHUNK):
         cut = slice(offset(level), offset(level) + 128 * (level + 1))
 
         def body(t, carry):
@@ -310,7 +316,7 @@
             answer[at, :] = answer[at, :] - change[:, 128 * level :]
             return carry
 
-        lax.fori_loop(0, ROWS // CHUNK, body, 0)
+        lax.fori_loop(start, end, body, 0)
 
     def turn(ref, first, count):
         for k in range(count):
@@ -323,10 +329,10 @@
 
     wait(ag_a)
     turn(fa, 1, 1)
-    inverse = inverse_of(block(fa, 0), 8.0)
     wait(rs_c)
     pc[c] = rc[me] + jnp.sum(rsc[...], axis=0)
     core_p = send(pc.at[c], pc.at[c], core_sem, 3, core_id)
+    inverse = inverse_of(block(fa, 0), 8.0)
     wait(ag_b)
     for k in range(2):
         mt[128 * k + 128 : 128 * k + 256, :] = block(fb, k).T
@@ -349,7 +355,7 @@
 
     z1.wait()
     inverse = inverse_of(z1s[...] + z1r[...], 4.0)
-    subtract(3)
+    subtract(3, 0, LATER)
     wait(ag_c)
     turn(fc, 0, 2)
     m21 = block(fc, 0)
@@ -361,7 +367,8 @@
     z2s[...] = block(fc, 3) - full
     z2 = send(z2s, z2r, z_sem, 2, z_ids[1])
     keep(2, dot_full(inverse, jnp.concatenate([m21, rest], axis=1)))
-    subtract(2)
+    subtract(3, LATER)
+    subtract(2, 0, LATER)
     z2p.wait()
     p1[...] = z2ps[...] + z2pr[...]
     fd[me] = p1[...]
@@ -369,6 +376,7 @@
 
     z2.wait()
     inverse = inverse_of(z2s[...] + z2r[...], 2.0)
+    subtract(2, LATER)
     wait(ag_d)
     turn(fd, 0, 1)
     m1 = blocks(fd, 0, 2)
@@ -427,7 +435,6 @@
         return pltpu.SemaphoreType.DMA((2, n))
 
     whole = pl.BlockSpec(memory_space=pltpu.VMEM)
-    scalar = pl.BlockSpec(memory_space=pltpu.SMEM)
     anywhere = pl.BlockSpec(memory_space=pl.ANY)
     results = [
         jax.ShapeDtypeStruct((4 * ROWS, CAP), F32),
@@ -440,12 +447,13 @@
 
     state = pl.pallas_call(
         kernel,
-        in_specs=[scalar, scalar, whole, anywhere, anywhere, anywhere, anywhere],
+        in_specs=[anywhere] * 7,
         out_specs=[anywhere] * 4 + [whole] * 2,
         out_shape=results + last,
         scratch_shapes=[
+            pltpu.SMEM((ROWS,), jnp.int32), pltpu.SMEM((ROWS,), F32), vmem(16, CAP),
             vmem(4 * ROWS, CAP), vmem(ROWS, 4, CAP), vmem(ROWS, CAP), vmem(ROWS, 1, CAP),
-            pltpu.SemaphoreType.DMA((10,)),
+            pltpu.SemaphoreType.DMA((13,)),
             vmem(4 * ROWS, CAP), vmem(ROWS, CAP), vmem(ROWS, CAP, dtype=BF), vmem(ROWS, CAP, dtype=BF),
             pltpu.SemaphoreType.DMA((4,)),
             vmem(ROWS, 640, dtype=BF), vmem(ROWS, 640, dtype=BF),

time: 63.3 us -> 62 us (0.979)
  Pallas kernels: 62.4 us -> 61.1 us
    pallas_call x1, Pallas kernels: 59.9 us -> 58.6 us  [local(): pl.pallas_call(kernel, in_specs=[anywhere] * 7, out_specs=[anywhere] * 4...]
where the time goes in v1:
time: 62 us; the launch traced here: 61.9 us
  Pallas kernels  61.1 us (99%)
  between operations  0.82 us (1%)
    pallas_call x1, Pallas kernels, local(): pl.pallas_call(kernel, in_specs=[anywhere] * 7, out_specs=[anywhere] * 4...  58.6 us
    pallas_call x1, Pallas kernels, local(): pl.pallas_call(finish_kernel, in_specs=[anywhere] + [whole] * 5, out_spec...  2.45 us

profile of v1, /device:TPU:24, one launch (start us, length us, event | category | flops | bytes accessed | tf_op | source)
XLA Modules:
  0.0 61.9 jit_solution(182731487273333833)
XLA Ops:
  0.6 58.6 %hodlr.1 = (f32[8192,128]{1,0:T(8,128)S(1)}, f32[2048,128]{1,0:T(8,128)S(1)}, bf16[2048,128]{1,0:T(8,128)(2,1)S(1)}, bf16[2048,128]{1,0:T(8,128)(2,1)S(1)}, bf16...) custom-call(s32[2048]{0:T(1024)} %bitcast.8, f32[2048]{0:T(1024)} %w_hbm.1, f32[16,128]{1,0:T(8,128)} %bitcast.7, ...), custom_call_target="tpu_custom_call" | custom-call | tf_op jit(solution)/shard_map/hodlr/pallas_call | solution.py:448
  59.2 2.5 %finish.1 = (f32[8192,128]{1,0:T(8,128)}, f32[2048,128]{1,0:T(8,128)}) custom-call(f32[8192,128]{1,0:T(8,128)S(1)} %get-tuple-element.10.applied_in, f32[2048,128]{1,0:T(8,128)S(1)} %get-tuple-element.11.answer_in, bf16[2048,128]{1,0:T(8,128)(2,1)S(1)} %get-tuple-element.12.a0h, bf16[2048,128]{1,0:T(8,128)(2,1)S(1)} %get-tuple-element.13.a0l, ...), custom_call_target="tpu_custom_call" | custom-call | tf_op jit(solution)/shard_map/finish/pallas_call | solution.py:484
